TPU v7x, 256 devices: a whole 4x4x8 slice. The times are simulated.
256 devices in a mesh: tok: 32 (over z, y_lo, core), tp: 8 (over y_hi, x).
Axes of the slice: x: 4, y: 4 (y_hi: 2, y_lo: 2; y = y_hi * 2 + y_lo), z: 8, core: 2. Of those that a mesh axis runs over, the one named last changes fastest.
Arguments:
- hidden_in: bfloat16 [8192, 4096], P('tok', 'tp'), may hold values from -6 to 6
- norm_gain: float32 [4096], replicated, may hold values from 0.5 to 9, as said below
- w_query: bfloat16 [4096, 4096], P(None, 'tp'), may hold values from -0.09375 to 0.09375
- w_key: bfloat16 [4096, 1024], P(None, 'tp'), may hold values from -0.09375 to 0.09375
- w_value: bfloat16 [4096, 1024], P(None, 'tp'), may hold values from -0.09375 to 0.09375
- w_out: bfloat16 [4096, 4096], P('tp'), may hold values from -0.5 to 0.5
- doc_ids: int32 [8192], replicated, may hold values from 0 to 3, never falling along the last dimension, each value on 1 to 6144 neighbouring positions
Outputs:
- hidden_out: bfloat16 [8192, 4096], P('tok', 'tp')
- joint_cov: float32 [2, 4096, 2, 4096], P(None, 'tok', None, 'tp')
Inputs may be any that keep to these rules, and one draw needn't show every extreme that they name: `norm_gain`: each channel's gain is positive. `doc_ids`: document numbers never fall along the tokens; a document holds 1 to 6144 tokens.
All inputs are finite; a program needn't handle non-finite values.
Results may differ from a plain program's by a relative error of at most 0.013.
The roundings to bfloat16 on the way count: a program that leaves them out, or rounds other values in their place, can miss the bound.
Values may be sent and summed in bfloat16 or wider, within the bound.
No kernel may reach another device: no remote copies, remote signals or barrier semaphores. Data moves between devices by JAX's collectives and lax.ppermute only.
A program may use at most 128 MiB of HBM per device.

v0:
```python
import jax
import jax.numpy as jnp
from jax import lax
from jax.sharding import PartitionSpec as P

HS = 128
epsilon = 1e-05
rope_base = 500000.0


def laid_out(blocks, dim):
    blocks = jnp.moveaxis(blocks, 0, dim)
    dims = blocks.shape
    return blocks.reshape(*dims[:dim], dims[dim] * dims[dim + 1], *dims[dim + 2 :])


def copy_for_each(x, axis):
    copies = jnp.broadcast_to(x, (lax.axis_size(axis), *x.shape))
    return lax.all_to_all(copies, axis, split_axis=0, concat_axis=0, tiled=True)


def collect(x, axis, dim):
    return laid_out(copy_for_each(x, axis), dim)


def in_one_piece(arrays, axis, dim, along):
    ends, at = ([], 0)
    for a in arrays[:-1]:
        at += a.shape[along]
        ends.append(at)
    both = jnp.concatenate(arrays, axis=along)
    return tuple(jnp.split(lax.all_gather(both, axis, axis=dim, tiled=True), ends, axis=along))


def rotate(vectors, positions):
    half_dim = vectors.shape[-1] // 2
    inv_freq = rope_base ** (-(jnp.arange(half_dim, dtype=jnp.float32) * 2.0) / vectors.shape[-1])
    angles = positions.astype(jnp.float32)[:, None] * inv_freq[None, :]
    cosine = jnp.cos(angles)[:, None, :]
    sine_part = jnp.sin(angles)[:, None, :]
    first_half = vectors[..., :half_dim]
    second_half = vectors[..., half_dim:]
    return jnp.concatenate(
        [
            first_half * cosine - second_half * sine_part,
            second_half * cosine + first_half * sine_part,
        ],
        axis=-1,
    )


def on_device(hidden_in, norm_gain, w_query, w_key, w_value, w_out, doc_ids):
    tok_rows = hidden_in.shape[0]
    col_width = hidden_in.shape[1]
    tok_count = lax.axis_size("tok")
    tok_index = lax.axis_index("tok")
    tp_index = lax.axis_index("tp")
    all_rows = tok_rows * tok_count
    full_in = collect(hidden_in, "tp", 1)
    model_width = full_in.shape[1]
    row_width = model_width // tok_count
    widened = full_in.astype(jnp.float32)
    factor = lax.rsqrt(jnp.mean(widened * widened, axis=1, keepdims=True) + epsilon)
    normed = (widened * factor * norm_gain[None, :]).astype(jnp.bfloat16)
    kv_heads = w_key.shape[1] // HS
    groups = w_query.shape[1] // w_key.shape[1]
    first_row = tok_index * tok_rows
    positions = first_row + jnp.arange(tok_rows, dtype=jnp.int32)
    key_local = rotate(
        jnp.dot(normed, w_key, preferred_element_type=jnp.float32).reshape(tok_rows, kv_heads, HS),
        positions % all_rows,
    )
    key_local = key_local.astype(jnp.bfloat16).reshape(tok_rows, kv_heads * HS)
    value_local = jnp.dot(normed, w_value, preferred_element_type=jnp.float32).astype(jnp.bfloat16)
    key_rows, value_rows = in_one_piece((key_local, value_local), "tok", 0, 1)
    queries = rotate(
        jnp.dot(normed, w_query, preferred_element_type=jnp.float32).reshape(
            tok_rows, kv_heads * groups, HS
        ),
        positions % all_rows,
    )
    queries = queries.astype(jnp.bfloat16).reshape(tok_rows, kv_heads, groups, HS)
    key_seq = key_rows.reshape(all_rows, kv_heads, HS)
    value_seq = value_rows.reshape(all_rows, kv_heads, HS)
    key_pos = jnp.arange(all_rows, dtype=jnp.int32)
    query_doc = lax.dynamic_slice_in_dim(doc_ids, first_row, tok_rows, 0)
    allowed = (query_doc[:, None] == doc_ids[None, :]) & (key_pos[None, :] <= positions[:, None])
    scores = jnp.einsum(
        "qhgd,khd->hgqk", queries, key_seq, preferred_element_type=jnp.float32
    ) * HS ** (-0.5)
    scores = jnp.where(allowed[None, None], scores, -jnp.inf)
    row_max = jnp.max(scores, axis=-1, keepdims=True)
    weights = jnp.exp(scores - row_max)
    weight_sum = jnp.sum(weights, axis=-1, keepdims=True)
    blended = (
        jnp.einsum(
            "hgqk,khd->hgqd",
            weights.astype(jnp.bfloat16),
            value_seq,
            preferred_element_type=jnp.float32,
        )
        / weight_sum
    )
    attended = (
        jnp.transpose(blended, (2, 0, 1, 3))
        .astype(jnp.bfloat16)
        .reshape(tok_rows, kv_heads * groups * HS)
    )
    partial_out = jnp.dot(attended, w_out, preferred_element_type=jnp.float32)
    summed = lax.psum(partial_out, "tp")
    full_out = (widened + summed).astype(jnp.bfloat16)
    hidden_out = lax.dynamic_slice_in_dim(full_out, tp_index * col_width, col_width, 1)
    joint_local = jnp.stack(
        [
            full_in.reshape(tok_rows, tok_count, row_width),
            full_out.reshape(tok_rows, tok_count, row_width),
        ],
        axis=1,
    )
    row_block = lax.all_to_all(joint_local, "tok", split_axis=2, concat_axis=0, tiled=True).reshape(
        all_rows, 2 * row_width
    )
    portion = lax.all_gather(jnp.stack([hidden_in, hidden_out], axis=1), "tok", axis=0, tiled=True)
    piece_rows = portion.shape[0]
    flat_part = portion.reshape(piece_rows, 2 * col_width)
    product = lax.dot_general(
        row_block, flat_part, (((0,), (0,)), ((), ())), preferred_element_type=jnp.float32
    )
    col_sum = jnp.sum(flat_part, axis=0, dtype=jnp.float32)
    row_mean = jnp.sum(row_block, axis=0, dtype=jnp.float32) / all_rows
    col_mean = col_sum / all_rows
    joint_cov = (product / all_rows - row_mean[:, None] * col_mean[None, :]).reshape(
        2, row_width, 2, col_width
    )
    return (hidden_out, joint_cov)


def solution(mesh):
    return jax.shard_map(
        on_device,
        mesh=mesh,
        in_specs=(
            P("tok", "tp"),
            P(),
            P(None, "tp"),
            P(None, "tp"),
            P(None, "tp"),
            P("tp", None),
            P(),
        ),
        out_specs=(P("tok", "tp"), P(None, "tok", None, "tp")),
        check_vma=False,
    )
```

profile of v0, /device:TPU:1, one launch (start us, length us, event | category | flops | bytes accessed | tf_op | source)
XLA Modules:
  0.0 543.1 jit_solution(12067020020564749845)
XLA Ops:
  9.8 7.5 %all-to-all-start = ((bf16[8,256,512]{1,2,0:T(8,128)(2,1)}), bf16[8,256,512]{1,2,0:T(8,128)(2,1)S(1)}, u32[]{:S(2)}, u32[]{:S(2)}) async-start(bf16[8,256,512]{1,2,0:T(8,128)(2,1)} %broadcast_in_dim.10), calls=%async_computation | async-start | bytes 4194304 | tf_op jit(solution)/shard_map/all_to_all | solution.py:19
  17.4 28.5 %all-to-all-done = bf16[8,256,512]{1,2,0:T(8,128)(2,1)S(1)} async-done(((bf16[8,256,512]{1,2,0:T(8,128)(2,1)}), bf16[8,256,512]{1,2,0:T(8,128)(2,1)S(1)}, u32[]{:S(2)}, u32[]{:S(2)}) %all-to-all-start) | async-done | bytes 2097184 | tf_op jit(solution)/shard_map/all_to_all | solution.py:19
  46.5 2.3 bitcast_convert_fusion
  48.8 5.7 %copy.44 = f32[256,4096]{1,0:T(8,128)} copy(f32[256,4096]{0,1:T(8,128)} %bitcast.92) | data formatting | bytes 8388608 | tf_op jit(solution)/shard_map/convert_element_type | solution.py:62
  54.4 2.9 multiply_convert_fusion.1
  60.3 6.4 %copy.47 = bf16[512,4096]{1,0:T(8,128)(2,1)} copy(bf16[512,4096]{0,1:T(8,128)(2,1)} %bitcast.95) | data formatting | bytes 8388608 | tf_op jit(solution)/shard_map/dot_general | solution.py:77
  67.1 4.7 fusion.7
  73.8 61.0 %all-gather.3.cloned.1.call-done = bf16[8192,256]{0,1:T(8,128)(2,1)} async-done(((bf16[256,256]{0,1:T(8,128)(2,1)}), bf16[8192,256]{0,1:T(8,128)(2,1)}) %all-gather.3.cloned.1.call-update) | async-done | bytes 4194320 | tf_op jit(solution)/shard_map/all_gather | solution.py:32
  134.9 15.3 %fusion.2 = (f32[4,256]{1,0:T(4,128)S(1)}, f32[8192,256,4]{1,0,2:T(8,128)}) fusion(pred[256,8192]{0,1:T(8,128)(4,1)} %fusion.7, bf16[256,4,64]{0,2,1:T(8,128)(2,1)S(1)} %get-tuple-element.3, bf16[256,4,64]{0,2,1:T(8,128)(2,1)S(1)} %get-tuple-element.2, bf16[8192,256]{0,1:T(8,128)(2,1)} %all-gather.3.cloned.1.call-done), kind=kOutput, calls=%fused_computation.5 | convolution fusion | flops 2173172736 | bytes 38014976 | tf_op jit(solution)/shard_map/qhgd,khd->hgqk/dot_general | solution.py:88
  150.2 14.5 %fusion = f32[4,256]{1,0:T(4,128)S(1)} fusion(f32[8192,256,4]{1,0,2:T(8,128)} %get-tuple-element.9, f32[4,256]{1,0:T(4,128)S(1)} %get-tuple-element.8, pred[256,8192]{0,1:T(8,128)(4,1)S(1)} %copy-done.3), kind=kLoop, calls=%fused_computation.3 | loop fusion | flops 33553408 | bytes 35659776 | tf_op jit(solution)/shard_map/reduce_sum | solution.py:94
  164.7 15.5 %fusion.13 = bf16[4,256,128]{1,2,0:T(8,128)(2,1)S(1)} fusion(f32[8192,256,4]{1,0,2:T(8,128)} %get-tuple-element.9, f32[4,256]{1,0:T(4,128)S(1)} %get-tuple-element.8, pred[256,8192]{0,1:T(8,128)(4,1)} %fusion.7, bf16[8192,256]{0,1:T(8,128)(2,1)} %all-gather.3.cloned.1.call-done, f32[4,256]{1,0:T(4,128)S(1)} %fusion), kind=kOutput, calls=%fused_computation.26 | convolution fusion | flops 2181300224 | bytes 38019072 | tf_op jit(solution)/shard_map/hgqk,khd->hgqd/dot_general | solution.py:96
  180.2 5.5 %fusion.35 = f32[256,4096]{1,0:T(8,128)} fusion(bf16[256,512]{0,1:T(8,128)(2,1)S(1)} %bitcast.100, bf16[512,4096]{1,0:T(8,128)(2,1)} %param.12), kind=kOutput, calls=%fused_computation.63 | convolution fusion | flops 1073741824 | bytes 8650752 | tf_op jit(solution)/shard_map/dot_general | solution.py:109
  185.7 113.2 %all-reduce.2.cloned.1.call-done = f32[256,4096]{1,0:T(8,128)} async-done(((f32[256,4096]{1,0:T(8,128)}), f32[256,4096]{1,0:T(8,128)}) %all-reduce.2.cloned.1.call-update) | async-done | bytes 4194320 | tf_op jit(solution)/shard_map/psum | solution.py:110
  298.9 4.0 add_convert_fusion
  305.1 4.1 copy.48
  313.5 7.9 %all-to-all-start.1 = ((bf16[256,2,32,128]{0,3,1,2:T(8,128)(2,1)}), bf16[256,2,32,128]{0,3,1,2:T(8,128)(2,1)}, u32[]{:S(2)}, u32[]{:S(2)}) async-start(bf16[256,2,32,128]{0,3,1,2:T(8,128)(2,1)} %copy.37), calls=%async_computation.1 | async-start | bytes 8388608 | tf_op jit(solution)/shard_map/all_to_all | solution.py:120
  323.1 139.7 %all-to-all-done.1 = bf16[256,2,32,128]{0,3,1,2:T(8,128)(2,1)} async-done(((bf16[256,2,32,128]{0,3,1,2:T(8,128)(2,1)}), bf16[256,2,32,128]{0,3,1,2:T(8,128)(2,1)}, u32[]{:S(2)}, u32[]{:S(2)}) %all-to-all-start.1) | async-done | bytes 4194336 | tf_op jit(solution)/shard_map/all_to_all | solution.py:120
  462.8 4.6 copy.38
  467.4 6.4 %copy.49 = bf16[32,8,32,256]{3,1,2,0:T(8,128)(2,1)} copy(bf16[32,8,32,256]{3,2,1,0:T(8,128)(2,1)S(1)} %bitcast.93) | data formatting | bytes 8388608
  473.8 2.9 convert_reduce_fusion.1
  476.7 17.3 %all-gather.5.cloned.1.call-done = bf16[8192,2,512]{2,0,1:T(8,128)(2,1)} async-done(((bf16[256,2,512]{2,0,1:T(8,128)(2,1)}), bf16[8192,2,512]{2,0,1:T(8,128)(2,1)}) %all-gather.5.cloned.1.call-update) | async-done | bytes 16777232 | tf_op jit(solution)/shard_map/all_gather | solution.py:123
  494.0 10.3 %convert_reduce_fusion = f32[2,512]{1,0:T(2,128)S(1)} fusion(bf16[8192,2,512]{2,0,1:T(8,128)(2,1)} %all-gather.5.cloned.1.call-done), kind=kLoop, calls=%fused_computation.1 | loop fusion | flops 16776192 | bytes 16781312 | tf_op jit(solution)/shard_map/reduce_sum | solution.py:129
  504.4 20.9 %copy.39 = bf16[8192,2,512]{0,2,1:T(8,128)(2,1)} copy(bf16[8192,2,512]{2,0,1:T(8,128)(2,1)} %all-gather.5.cloned.1.call-done) | data formatting | bytes 33554432 | tf_op jit(solution)/shard_map/all_gather | solution.py:123
  525.3 9.4 %fusion.9 = f32[256,1024]{1,0:T(8,128)S(1)} fusion(bf16[8192,256]{0,1:T(8,128)(2,1)} %bitcast.97, bf16[8192,1024]{0,1:T(8,128)(2,1)} %bitcast.91, f32[1024]{0:T(1024)S(1)} %bitcast.101, f32[256]{0:T(256)S(1)} %multiply_bitcast_fusion.1), kind=kOutput, calls=%fused_computation.22 | convolution fusion | flops 4295753728 | bytes 22025216 | tf_op jit(solution)/shard_map/dot_general | solution.py:126
  (50 shorter events, 18.7 us)
Async XLA Ops:
  7.2 50.1 %copy-start = (bf16[4096,128]{1,0:T(8,128)(2,1)S(1)}, bf16[4096,128]{1,0:T(8,128)(2,1)}, u32[]{:S(2)}) copy-start(bf16[4096,128]{1,0:T(8,128)(2,1)} %param.11) | copy-start | bytes 3145732
  9.8 36.0 %all-to-all-start = ((bf16[8,256,512]{1,2,0:T(8,128)(2,1)}), bf16[8,256,512]{1,2,0:T(8,128)(2,1)S(1)}, u32[]{:S(2)}, u32[]{:S(2)}) async-start(bf16[8,256,512]{1,2,0:T(8,128)(2,1)} %broadcast_in_dim.10), calls=%async_computation | async-start | bytes 4194304 | tf_op jit(solution)/shard_map/all_to_all | solution.py:19
  17.3 117.6 %all-gather.3.cloned.1.call-start = ((), (), s32[]{:S(2)}) async-start(), calls=%async_computation.2 | async-start | bytes 4325376 | tf_op jit(solution)/shard_map/all_gather | solution.py:32
  48.8 5.7 %copy-start.7 = (f32[4096]{0:T(1024)S(1)}, f32[4096]{0:T(1024)}, u32[]{:S(2)}) copy-start(f32[4096]{0:T(1024)} %param.8) | copy-start | bytes 49156
  54.4 3.7 copy-start.5
  60.0 238.9 %all-reduce.2.cloned.1.call-start = ((), (), s32[]{:S(2)}) async-start(), calls=%async_computation.3 | async-start | bytes 8388608 | tf_op jit(solution)/shard_map/psum | solution.py:110
  60.2 6.5 %copy-start.8 = (s32[8192]{0:T(1024)S(1)}, s32[8192]{0:T(1024)}, u32[]{:S(2)}) copy-start(s32[8192]{0:T(1024)} %param.13) | copy-start | bytes 98308
  66.7 5.8 %copy-start.4 = (bf16[512,4096]{1,0:T(8,128)(2,1)S(1)}, bf16[512,4096]{1,0:T(8,128)(2,1)}, u32[]{:S(2)}) copy-start(bf16[512,4096]{1,0:T(8,128)(2,1)} %copy.47) | copy-start | bytes 12582916
  134.9 15.3 %copy-start.3 = (pred[256,8192]{0,1:T(8,128)(4,1)S(1)}, pred[256,8192]{0,1:T(8,128)(4,1)}, u32[]{:S(2)}) copy-start(pred[256,8192]{0,1:T(8,128)(4,1)} %fusion.7) | copy-start | bytes 6291460
  185.6 308.4 %all-gather.5.cloned.1.call-start = ((), (), s32[]{:S(2)}) async-start(), calls=%async_computation.4 | async-start | bytes 17301504 | tf_op jit(solution)/shard_map/all_gather | solution.py:123
  185.7 118.6 %copy-start.6 = (bf16[256,512]{1,0:T(8,128)(2,1)S(1)}, bf16[256,512]{1,0:T(8,128)(2,1)}, u32[]{:S(2)}) copy-start(bf16[256,512]{1,0:T(8,128)(2,1)} %param.7) | copy-start | bytes 786436
  302.9 1.4 copy-start.2
  313.5 149.3 %all-to-all-start.1 = ((bf16[256,2,32,128]{0,3,1,2:T(8,128)(2,1)}), bf16[256,2,32,128]{0,3,1,2:T(8,128)(2,1)}, u32[]{:S(2)}, u32[]{:S(2)}) async-start(bf16[256,2,32,128]{0,3,1,2:T(8,128)(2,1)} %copy.37), calls=%async_computation.1 | async-start | bytes 8388608 | tf_op jit(solution)/shard_map/all_to_all | solution.py:120
  525.3 11.3 %copy-start.1 = (bf16[4096,128]{1,0:T(8,128)(2,1)S(1)}, bf16[4096,128]{1,0:T(8,128)(2,1)}, u32[]{:S(2)}) copy-start(bf16[4096,128]{1,0:T(8,128)(2,1)} %param.11) | copy-start | bytes 3145732
Sparse Core Ops, SparseCore 0:
  60.1 74.7 all-gather.2
  185.8 113.0 all-reduce.1
  305.3 188.7 all-gather.4
where the time goes:
time: 544 us; the launch traced here: 543 us
  waiting for transfers between devices  360 us (66%)
  local copies, waits for them, and re-layouts  58 us (11%)
  matrix products  48.6 us (9%)
  other arithmetic  47.1 us (9%)
  starting transfers between devices  15.7 us (3%)
  between operations  14 us (3%)
    all_to_all x1, waiting for transfers between devices, on_device(): lax.all_to_all(joint_local, 'tok', split_axis=2, concat_axis=0, tiled=True)  140 us
    psum x1, waiting for transfers between devices, on_device(): summed = lax.psum(partial_out, 'tp')  113 us
    all_gather x1, waiting for transfers between devices, in_one_piece(): lax.all_gather(both, axis, axis=dim, tiled=True)  61 us
    all_to_all x1, waiting for transfers between devices, copy_for_each(): return lax.all_to_all(copies, axis, split_axis=0, concat_axis=0, tiled=True)  28.5 us
    all_gather x1, local copies, waits for them, and re-layouts, on_device(): lax.all_gather(jnp.stack([hidden_in, hidden_out], axis=1), 'tok', axis=0,...  20.9 us
    all_gather x1, waiting for transfers between devices, on_device(): lax.all_gather(jnp.stack([hidden_in, hidden_out], axis=1), 'tok', axis=0,...  17.3 us
    dot_general x1, matrix products, on_device(): jnp.einsum('hgqk,khd->hgqd', weights.astype(jnp.bfloat16), value_seq, pre...  15.5 us
    dot_general x1, matrix products, on_device(): jnp.einsum('qhgd,khd->hgqk', queries, key_seq, preferred_element_type=jnp...  15.3 us
  transfers between devices with their start and end apart: 5, of which 5 were waited for; matrix products, arithmetic and copies ran while one was open for 7% of the time, Pallas kernels for 0%

commit v1 on v0

--- a/solution.py
+++ b/solution.py
@@ -117,9 +117,12 @@
         ],
         axis=1,
     )
-    row_block = lax.all_to_all(joint_local, "tok", split_axis=2, concat_axis=0, tiled=True).reshape(
-        all_rows, 2 * row_width
-    )
+    row_block = jnp.concatenate(
+        lax.all_to_all(
+            jnp.stack(jnp.split(joint_local, lax.axis_size("tok"), axis=2)), "tok", 0, 0
+        ),
+        axis=0,
+    ).reshape(all_rows, 2 * row_width)
     portion = lax.all_gather(jnp.stack([hidden_in, hidden_out], axis=1), "tok", axis=0, tiled=True)
     piece_rows = portion.shape[0]
     flat_part = portion.reshape(piece_rows, 2 * col_width)

time: 544 us -> 546 us (level)
  other arithmetic: 47.1 us -> 67.3 us
  waiting for transfers between devices: 360 us -> 343 us
    unnamed x1 -> x32, other arithmetic: 0.01 us -> 21.6 us
    all_gather x1, waiting for transfers between devices: 17.3 us -> 0.02 us  [on_device(): lax.all_gather(jnp.stack([hidden_in, hidden_out], axis=1), 'tok', axis=0,...]
  transfers between devices with their start and end apart: 5 -> 5, of which waited for: 5 -> 4; matrix products, arithmetic and copies ran while one was open for 7% -> 10% of each run, Pallas kernels for 0% -> 0%
where the time goes in v1:
time: 546 us; the launch traced here: 544 us
  waiting for transfers between devices  343 us (63%)
  other arithmetic  67.3 us (12%)
  local copies, waits for them, and re-layouts  56.3 us (10%)
  matrix products  48.6 us (9%)
  starting transfers between devices  15.7 us (3%)
  between operations  14 us (3%)
    all_to_all x1, waiting for transfers between devices, on_device(): lax.all_to_all(jnp.stack(jnp.split(joint_local, lax.axis_size('tok'), axi...  140 us
    psum x1, waiting for transfers between devices, on_device(): summed = lax.psum(partial_out, 'tp')  113 us
    all_gather x1, waiting for transfers between devices, in_one_piece(): lax.all_gather(both, axis, axis=dim, tiled=True)  61.1 us
    all_to_all x1, waiting for transfers between devices, copy_for_each(): return lax.all_to_all(copies, axis, split_axis=0, concat_axis=0, tiled=True)  28.5 us
    unnamed x32, other arithmetic  21.6 us
    all_gather x1, local copies, waits for them, and re-layouts, on_device(): lax.all_gather(jnp.stack([hidden_in, hidden_out], axis=1), 'tok', axis=0,...  21.4 us
    dot_general x1, matrix products, on_device(): jnp.einsum('hgqk,khd->hgqd', weights.astype(jnp.bfloat16), value_seq, pre...  15.5 us
    dot_general x1, matrix products, on_device(): jnp.einsum('qhgd,khd->hgqk', queries, key_seq, preferred_element_type=jnp...  15.3 us
  transfers between devices with their start and end apart: 5, of which 4 were waited for; matrix products, arithmetic and copies ran while one was open for 10% of the time, Pallas kernels for 0%

profile of v1, /device:TPU:1, one launch (start us, length us, event | category | flops | bytes accessed | tf_op | source)
XLA Modules:
  0.0 544.3 jit_solution(2448292159534658929)
XLA Ops:
  9.8 7.5 %all-to-all-start = ((bf16[8,256,512]{1,2,0:T(8,128)(2,1)}), bf16[8,256,512]{1,2,0:T(8,128)(2,1)S(1)}, u32[]{:S(2)}, u32[]{:S(2)}) async-start(bf16[8,256,512]{1,2,0:T(8,128)(2,1)} %broadcast_in_dim.10), calls=%async_computation | async-start | bytes 4194304 | tf_op jit(solution)/shard_map/all_to_all | solution.py:19
  17.4 28.5 %all-to-all-done = bf16[8,256,512]{1,2,0:T(8,128)(2,1)S(1)} async-done(((bf16[8,256,512]{1,2,0:T(8,128)(2,1)}), bf16[8,256,512]{1,2,0:T(8,128)(2,1)S(1)}, u32[]{:S(2)}, u32[]{:S(2)}) %all-to-all-start) | async-done | bytes 2097184 | tf_op jit(solution)/shard_map/all_to_all | solution.py:19
  46.5 2.3 bitcast_convert_fusion
  48.8 5.7 %copy.127 = f32[256,4096]{1,0:T(8,128)} copy(f32[256,4096]{0,1:T(8,128)} %bitcast.277) | data formatting | bytes 8388608 | tf_op jit(solution)/shard_map/convert_element_type | solution.py:62
  54.5 2.9 multiply_convert_fusion.1
  60.3 6.4 %copy.130 = bf16[512,4096]{1,0:T(8,128)(2,1)} copy(bf16[512,4096]{0,1:T(8,128)(2,1)} %bitcast.279) | data formatting | bytes 8388608 | tf_op jit(solution)/shard_map/dot_general | solution.py:77
  67.1 4.7 fusion.7
  73.8 61.1 %all-gather.3.cloned.1.call-done = bf16[8192,256]{0,1:T(8,128)(2,1)} async-done(((bf16[256,256]{0,1:T(8,128)(2,1)}), bf16[8192,256]{0,1:T(8,128)(2,1)}) %all-gather.3.cloned.1.call-update) | async-done | bytes 4194320 | tf_op jit(solution)/shard_map/all_gather | solution.py:32
  134.9 15.3 %fusion.2 = (f32[4,256]{1,0:T(4,128)S(1)}, f32[8192,256,4]{1,0,2:T(8,128)}) fusion(pred[256,8192]{0,1:T(8,128)(4,1)} %fusion.7, bf16[256,4,64]{0,2,1:T(8,128)(2,1)S(1)} %get-tuple-element.3, bf16[256,4,64]{0,2,1:T(8,128)(2,1)S(1)} %get-tuple-element.2, bf16[8192,256]{0,1:T(8,128)(2,1)} %all-gather.3.cloned.1.call-done), kind=kOutput, calls=%fused_computation.5 | convolution fusion | flops 2173172736 | bytes 38014976 | tf_op jit(solution)/shard_map/qhgd,khd->hgqk/dot_general | solution.py:88
  150.2 14.5 %fusion = f32[4,256]{1,0:T(4,128)S(1)} fusion(f32[8192,256,4]{1,0,2:T(8,128)} %get-tuple-element.9, f32[4,256]{1,0:T(4,128)S(1)} %get-tuple-element.8, pred[256,8192]{0,1:T(8,128)(4,1)S(1)} %copy-done.4), kind=kLoop, calls=%fused_computation.3 | loop fusion | flops 33553408 | bytes 35659776 | tf_op jit(solution)/shard_map/reduce_sum | solution.py:94
  164.7 15.5 %fusion.13 = bf16[4,256,128]{1,2,0:T(8,128)(2,1)S(1)} fusion(f32[8192,256,4]{1,0,2:T(8,128)} %get-tuple-element.9, f32[4,256]{1,0:T(4,128)S(1)} %get-tuple-element.8, pred[256,8192]{0,1:T(8,128)(4,1)} %fusion.7, bf16[8192,256]{0,1:T(8,128)(2,1)} %all-gather.3.cloned.1.call-done, f32[4,256]{1,0:T(4,128)S(1)} %fusion), kind=kOutput, calls=%fused_computation.87 | convolution fusion | flops 2181300224 | bytes 38019072 | tf_op jit(solution)/shard_map/hgqk,khd->hgqd/dot_general | solution.py:96
  180.2 5.4 %fusion.68 = f32[256,4096]{1,0:T(8,128)} fusion(bf16[256,512]{0,1:T(8,128)(2,1)S(1)} %bitcast.284, bf16[512,4096]{1,0:T(8,128)(2,1)} %param.12), kind=kOutput, calls=%fused_computation.189 | convolution fusion | flops 1073741824 | bytes 8650752 | tf_op jit(solution)/shard_map/dot_general | solution.py:109
  185.7 113.2 %all-reduce.2.cloned.1.call-done = f32[256,4096]{1,0:T(8,128)} async-done(((f32[256,4096]{1,0:T(8,128)}), f32[256,4096]{1,0:T(8,128)}) %all-reduce.2.cloned.1.call-update) | async-done | bytes 4194320 | tf_op jit(solution)/shard_map/psum | solution.py:110
  298.9 4.0 add_convert_fusion
  305.1 4.1 copy.131
  331.5 7.9 %all-to-all-start.1 = ((bf16[32,256,2,1,128]{1,4,2,3,0:T(8,128)(2,1)}), bf16[32,256,2,1,128]{1,4,2,3,0:T(8,128)(2,1)}, u32[]{:S(2)}, u32[]{:S(2)}) async-start(bf16[32,256,2,1,128]{1,4,2,3,0:T(8,128)(2,1)} %fusion.51), calls=%async_computation.1 | async-start | bytes 8388608 | tf_op jit(solution)/shard_map/all_to_all | solution.py:121
  341.1 139.7 %all-to-all-done.1 = bf16[32,256,2,1,128]{1,4,2,3,0:T(8,128)(2,1)} async-done(((bf16[32,256,2,1,128]{1,4,2,3,0:T(8,128)(2,1)}), bf16[32,256,2,1,128]{1,4,2,3,0:T(8,128)(2,1)}, u32[]{:S(2)}, u32[]{:S(2)}) %all-to-all-start.1) | async-done | bytes 4194336 | tf_op jit(solution)/shard_map/all_to_all | solution.py:121
  480.8 4.6 copy.121
  485.5 6.4 %copy.163 = bf16[32,8,32,256]{3,1,2,0:T(8,128)(2,1)} copy(bf16[32,8,32,256]{3,2,1,0:T(8,128)(2,1)S(1)} %bitcast.278) | data formatting | bytes 8388608
  491.8 2.9 convert_reduce_fusion.1
  494.7 10.3 %convert_reduce_fusion = f32[2,512]{1,0:T(2,128)S(1)} fusion(bf16[8192,2,512]{2,0,1:T(8,128)(2,1)} %all-gather.5.cloned.1.call-done), kind=kLoop, calls=%fused_computation.1 | loop fusion | flops 16776192 | bytes 16781312 | tf_op jit(solution)/shard_map/reduce_sum | solution.py:132
  505.1 21.4 %copy.122 = bf16[8192,2,512]{0,2,1:T(8,128)(2,1)} copy(bf16[8192,2,512]{2,0,1:T(8,128)(2,1)} %all-gather.5.cloned.1.call-done) | data formatting | bytes 33554432 | tf_op jit(solution)/shard_map/all_gather | solution.py:126
  526.5 9.4 %fusion.9 = f32[256,1024]{1,0:T(8,128)S(1)} fusion(bf16[8192,256]{0,1:T(8,128)(2,1)} %bitcast.281, bf16[8192,1024]{0,1:T(8,128)(2,1)} %bitcast.276, f32[1024]{0:T(1024)S(1)} %bitcast.285, f32[256]{0:T(256)S(1)} %multiply_bitcast_fusion.1), kind=kOutput, calls=%fused_computation.83 | convolution fusion | flops 4295753728 | bytes 22025216 | tf_op jit(solution)/shard_map/dot_general | solution.py:129
  535.9 1.9 reshape.278
  (82 shorter events, 34.9 us)
Async XLA Ops:
  7.2 50.2 %copy-start = (bf16[4096,128]{1,0:T(8,128)(2,1)S(1)}, bf16[4096,128]{1,0:T(8,128)(2,1)}, u32[]{:S(2)}) copy-start(bf16[4096,128]{1,0:T(8,128)(2,1)} %param.11) | copy-start | bytes 3145732
  9.8 36.0 %all-to-all-start = ((bf16[8,256,512]{1,2,0:T(8,128)(2,1)}), bf16[8,256,512]{1,2,0:T(8,128)(2,1)S(1)}, u32[]{:S(2)}, u32[]{:S(2)}) async-start(bf16[8,256,512]{1,2,0:T(8,128)(2,1)} %broadcast_in_dim.10), calls=%async_computation | async-start | bytes 4194304 | tf_op jit(solution)/shard_map/all_to_all | solution.py:19
  17.3 117.6 %all-gather.3.cloned.1.call-start = ((), (), s32[]{:S(2)}) async-start(), calls=%async_computation.2 | async-start | bytes 4325376 | tf_op jit(solution)/shard_map/all_gather | solution.py:32
  48.8 5.7 %copy-start.8 = (f32[4096]{0:T(1024)S(1)}, f32[4096]{0:T(1024)}, u32[]{:S(2)}) copy-start(f32[4096]{0:T(1024)} %param.8) | copy-start | bytes 49156
  54.5 3.7 copy-start.6
  60.0 238.8 %all-reduce.2.cloned.1.call-start = ((), (), s32[]{:S(2)}) async-start(), calls=%async_computation.3 | async-start | bytes 8388608 | tf_op jit(solution)/shard_map/psum | solution.py:110
  60.3 6.4 %copy-start.9 = (s32[8192]{0:T(1024)S(1)}, s32[8192]{0:T(1024)}, u32[]{:S(2)}) copy-start(s32[8192]{0:T(1024)} %param.13) | copy-start | bytes 98308
  66.7 5.8 %copy-start.5 = (bf16[512,4096]{1,0:T(8,128)(2,1)S(1)}, bf16[512,4096]{1,0:T(8,128)(2,1)}, u32[]{:S(2)}) copy-start(bf16[512,4096]{1,0:T(8,128)(2,1)} %copy.130) | copy-start | bytes 12582916
  134.9 15.3 %copy-start.4 = (pred[256,8192]{0,1:T(8,128)(4,1)S(1)}, pred[256,8192]{0,1:T(8,128)(4,1)}, u32[]{:S(2)}) copy-start(pred[256,8192]{0,1:T(8,128)(4,1)} %fusion.7) | copy-start | bytes 6291460
  185.6 309.1 %all-gather.5.cloned.1.call-start = ((), (), s32[]{:S(2)}) async-start(), calls=%async_computation.4 | async-start | bytes 17301504 | tf_op jit(solution)/shard_map/all_gather | solution.py:126
  185.7 118.5 %copy-start.7 = (bf16[256,512]{1,0:T(8,128)(2,1)S(1)}, bf16[256,512]{1,0:T(8,128)(2,1)}, u32[]{:S(2)}) copy-start(bf16[256,512]{1,0:T(8,128)(2,1)} %param.7) | copy-start | bytes 786436
  302.8 1.4 copy-start.3
  309.2 1.6 copy-start.2
  331.5 149.3 %all-to-all-start.1 = ((bf16[32,256,2,1,128]{1,4,2,3,0:T(8,128)(2,1)}), bf16[32,256,2,1,128]{1,4,2,3,0:T(8,128)(2,1)}, u32[]{:S(2)}, u32[]{:S(2)}) async-start(bf16[32,256,2,1,128]{1,4,2,3,0:T(8,128)(2,1)} %fusion.51), calls=%async_computation.1 | async-start | bytes 8388608 | tf_op jit(solution)/shard_map/all_to_all | solution.py:121
  526.5 11.3 %copy-start.1 = (bf16[4096,128]{1,0:T(8,128)(2,1)S(1)}, bf16[4096,128]{1,0:T(8,128)(2,1)}, u32[]{:S(2)}) copy-start(bf16[4096,128]{1,0:T(8,128)(2,1)} %param.11) | copy-start | bytes 3145732
Sparse Core Ops, SparseCore 0:
  60.2 74.7 all-gather.2
  185.8 113.0 all-reduce.1
  305.2 188.7 all-gather.4
